TPU v7x, 32 devices: a whole 2x2x4 slice. The times are simulated.
32 devices in a mesh: track: 8 (over y, x, core), width: 4 (over z).
Axes of the slice: x: 2, y: 2, z: 4, core: 2. Of those that a mesh axis runs over, the one named last changes fastest.
Arguments:
- phase: float32 [256, 256, 512], P('track', 'width'), may hold values from -1 to 1
- solute: float32 [256, 256, 512], P('track', 'width'), may hold values from -0.5 to 0.5
- heat_rows: float32 [2048, 512], P(('track', 'width')), may hold values from -4 to 4
- rate_rows: float32 [2048, 512], P(('track', 'width')), may hold values from -6 to 6
- dest_tile: int32 [2048, 1], P(('track', 'width')), may hold values from 0 to 31; in each aligned block of 64 rows (0 to 63, 64 to 127, ...) at most 4 rows name the same one
- dest_block: int32 [2048], P(('track', 'width')), may hold values from 0 to 31
- active: int32 [32, 32], P('track', 'width'), may hold values 0 or 1
Outputs:
- phase_out: float32 [256, 256, 512], P('track', 'width')
- solute_out: float32 [256, 256, 512], P('track', 'width')
Inputs may be any that keep to these rules, and one draw needn't show every extreme that they name: `dest_tile`: the rows of one device send at most 4 rows to one tile, and exactly 4 to some tile.
All inputs are finite; a program needn't handle non-finite values. No bound on the sum of `active` on one device may be relied on, other than what follows from the above.
Results may differ from a plain program's by a relative error of at most 0.0003.
Values sent between devices are 32-bit elements; how exact they have to be, the bound alone decides.
A program may use at most 128 MiB of HBM per device.

v0:
```python
import jax
import jax.numpy as jnp
from jax import lax
from jax.sharding import PartitionSpec as P

BS = 8
STEPS = 3
CAP = 4


coef_track = 0.9
coef_width = 0.6
coef_depth = 0.35
time_step = 0.1
coupling = 1.6
diffusion = 0.8


def extended_2(cells, sides, width):
    for axis, dim in sides:
        count = lax.axis_size(axis)
        ends = count - 1
        head = lax.slice_in_dim(cells, 0, width, axis=dim)
        tail = lax.slice_in_dim(cells, cells.shape[dim] - width, cells.shape[dim], axis=dim)
        cells = jnp.concatenate(
            [
                lax.ppermute(tail, axis, [(i, (i + 1) % count) for i in range(ends)]),
                cells,
                lax.ppermute(head, axis, [((i + 1) % count, i) for i in range(ends)]),
            ],
            axis=dim,
        )
    return cells


def laplace(padded, along_first, along_second, along_third):
    depth_pad = jnp.pad(padded, ((0, 0), (0, 0), (1, 1)))
    center = padded[1:-1, 1:-1, :]
    first = padded[2:, 1:-1, :] + padded[:-2, 1:-1, :] - 2.0 * center
    second = padded[1:-1, 2:, :] + padded[1:-1, :-2, :] - 2.0 * center
    third = depth_pad[1:-1, 1:-1, 2:] + depth_pad[1:-1, 1:-1, :-2] - 2.0 * center
    return along_first * first + along_second * second + along_third * third


def advance(phase_ext, solute_ext, heat, rate, cells, count):
    inner_phase = phase_ext[1:-1, 1:-1, :]
    inner_solute = solute_ext[1:-1, 1:-1, :]
    theta = heat - count * time_step * rate
    bond = 1.0 - inner_phase * inner_phase
    drive = (
        laplace(phase_ext, coef_track, coef_width, coef_depth)
        + inner_phase
        - inner_phase * inner_phase * inner_phase
        - coupling * bond * bond * (theta + inner_solute)
    )
    change = cells * drive
    new_phase = inner_phase + time_step * change
    new_solute = inner_solute + time_step * (
        diffusion * laplace(solute_ext, 1.0, 1.0, 1.0) + 0.5 * change
    )
    return (new_phase, new_solute)


def expand(blocks, size):
    return jnp.repeat(jnp.repeat(blocks, size, axis=0), size, axis=1)


def on_device(phase, solute, heat_rows, rate_rows, dest_tile, dest_block, active):
    devices = lax.axis_size(("track", "width"))
    depth = heat_rows.shape[1]
    tile_x = phase.shape[0]
    tile_y = phase.shape[1]
    blocks_x = tile_x // BS
    blocks_y = tile_y // BS
    target = dest_tile[:, 0]
    hits = (target[:, None] == jnp.arange(devices, dtype=jnp.int32)[None, :]).astype(jnp.int32)
    earlier = jnp.cumsum(hits, axis=0) - hits
    placing = jnp.sum(earlier * hits, axis=1)
    slot = target * CAP + placing
    payload = jnp.concatenate([heat_rows, rate_rows], axis=1)
    outgoing = jnp.zeros((devices * CAP, 2 * depth), jnp.float32).at[slot].set(payload)
    labels = jnp.full((devices * CAP,), -1, jnp.int32).at[slot].set(dest_block)
    arrived, arrived_labels = (
        lax.all_to_all(
            outgoing.reshape(devices, CAP, 2 * depth),
            ("track", "width"),
            split_axis=0,
            concat_axis=0,
            tiled=True,
        ),
        lax.all_to_all(
            labels.reshape(devices, CAP),
            ("track", "width"),
            split_axis=0,
            concat_axis=0,
            tiled=True,
        ),
    )
    arrived = arrived.reshape(devices * CAP, 2 * depth)
    arrived_labels = arrived_labels.reshape(devices * CAP)
    selector = (
        jnp.arange(blocks_x * blocks_y, dtype=jnp.int32)[:, None] == arrived_labels[None, :]
    ).astype(jnp.float32)
    block_sums = jnp.dot(
        selector, arrived, precision=lax.Precision.HIGHEST, preferred_element_type=jnp.float32
    )
    block_sums = block_sums.reshape(blocks_x, blocks_y, 2, depth)
    heat = expand(block_sums[:, :, 0, :], BS)
    rate = expand(block_sums[:, :, 1, :], BS)
    cells = expand(active.astype(jnp.float32), BS)[:, :, None]
    for count in range(STEPS):
        extended = extended_2(jnp.stack([phase, solute]), (("track", 1), ("width", 2)), 1)
        phase, solute = advance(extended[0], extended[1], heat, rate, cells, count)
    return (phase, solute)


def solution(mesh):
    return jax.shard_map(
        on_device,
        mesh=mesh,
        in_specs=(
            P("track", "width", None),
            P("track", "width", None),
            P(("track", "width"), None),
            P(("track", "width"), None),
            P(("track", "width"), None),
            P(("track", "width")),
            P("track", "width"),
        ),
        out_specs=(P("track", "width", None), P("track", "width", None)),
        check_vma=False,
    )
```

profile of v0, /device:TPU:12, one launch (start us, length us, event | category | flops | bytes accessed | tf_op | source)
XLA Modules:
  0.0 201.7 jit_solution(12876542861644642305)
XLA Ops:
  3.7 4.5 %collective-permute-start.1 = (f32[2,1,64,512]{3,2,1,0:T(8,128)S(1)}, f32[2,1,64,512]{3,2,1,0:T(8,128)S(1)}, u32[]{:S(2)}, u32[]{:S(2)}) collective-permute-start(f32[2,1,64,512]{3,2,1,0:T(8,128)S(1)} %get-tuple-element.25), channel_id=1, source_target_pairs={{4,0},{8,4},{12,8},{16,12},{20,16},{24,20},{28,24},{5,1},{9,5},{13... | collective-permute-start | bytes 786440 | tf_op jit(solution)/shard_map/ppermute | solution.py:29
  10.3 5.1 %all-to-all-start = ((s32[32,1,4]{2,1,0:T(1,128)}), s32[32,1,4]{2,1,0:T(1,128)S(1)}, u32[]{:S(2)}, u32[]{:S(2)}) async-start(s32[32,1,4]{2,1,0:T(1,128)} %bitcast.7), calls=%async_computation | async-start | bytes 32768 | tf_op jit(solution)/shard_map/all_to_all | solution.py:91
  17.5 3.4 %collective-permute-start.2 = (f32[2,34,1,512]{3,2,1,0:T(1,128)S(1)}, f32[2,34,1,512]{3,2,1,0:T(1,128)S(1)}, u32[]{:S(2)}, u32[]{:S(2)}) collective-permute-start(f32[2,34,1,512]{3,2,1,0:T(1,128)S(1)} %get-tuple-element.18), channel_id=1, source_target_pairs={{0,1},{1,2},{2,3},{4,5},{5,6},{6,7},{8,9},{9,10},{10,11},{12,13},{... | collective-permute-start | bytes 417800 | tf_op jit(solution)/shard_map/ppermute | solution.py:27
  25.4 5.8 %all-to-all-start.1 = ((f32[32,4,1024]{2,1,0:T(4,128)}), f32[32,4,1024]{2,1,0:T(4,128)S(1)}, u32[]{:S(2)}, u32[]{:S(2)}) async-start(f32[32,4,1024]{2,1,0:T(4,128)} %reshape.73), calls=%async_computation.1 | async-start | bytes 1048576 | tf_op jit(solution)/shard_map/all_to_all | solution.py:84
  32.5 6.0 %pad_maximum_fusion = f32[2,34,66,512]{3,2,1,0:T(8,128)S(1)} fusion(f32[2,34,1,512]{3,2,1,0:T(1,128)S(1)} %collective-permute-done.3, f32[2,1,64,512]{3,2,1,0:T(8,128)S(1)} %collective-permute-done.1, f32[1,32,64,512]{3,2,1,0:T(8,128)} %bitcast.72, f32[1,32,64,512]{3,2,1,0:T(8,128)} %bitcast.75, f32[2,1,64,512]{3,2,1,0:T(8,128)S(1)} %collective-permute-done, ...), kind=kLoop, calls=%fused_computation.2 | loop fusion | flops 11489280 | bytes 18382848 | tf_op jit(solution)/shard_map/concatenate | solution.py:25
  38.6 5.0 %slice_bitcast_fusion.5 = (f32[34,66,512]{2,1,0:T(8,128)}, f32[34,66,512]{2,1,0:T(8,128)}) fusion(f32[2,34,66,512]{3,2,1,0:T(8,128)S(1)} %pad_maximum_fusion), kind=kLoop, calls=%fused_computation.31 | loop fusion | bytes 18382848 | tf_op jit(solution)/shard_map/squeeze | solution.py:113
  47.7 21.1 %add_bitcast_fusion.1 = (f32[1,32,64,512]{3,2,1,0:T(8,128)}, f32[32,64,512]{2,1,0:T(8,128)}) fusion(f32[34,66,512]{2,1,0:T(8,128)} %get-tuple-element.12, f32[34,66,512]{2,1,0:T(8,128)} %get-tuple-element.13, f32[32,8,512]{2,1,0:T(8,128)} %bitcast.77, f32[32,64]{1,0:T(8,128)S(1)} %copy.13), kind=kLoop, calls=%fused_computation.123 | loop fusion | flops 26214400 | bytes 39100416 | tf_op jit(solution)/shard_map/stack | solution.py:112
  68.9 9.3 %fusion.24 = f32[1,32,64,512]{3,2,1,0:T(8,128)} fusion(f32[34,66,512]{2,1,0:T(8,128)S(1)} %bitcast.69, f32[32,64,512]{2,1,0:T(8,128)} %get-tuple-element.7), kind=kLoop, calls=%fused_computation.56 | loop fusion | flops 14680064 | bytes 34373632 | tf_op jit(solution)/shard_map/stack | solution.py:112
  81.4 4.5 %collective-permute-start.5 = (f32[2,1,64,512]{3,2,1,0:T(8,128)S(1)}, f32[2,1,64,512]{3,2,1,0:T(8,128)S(1)}, u32[]{:S(2)}, u32[]{:S(2)}) collective-permute-start(f32[2,1,64,512]{3,2,1,0:T(8,128)S(1)} %get-tuple-element.23), channel_id=1, source_target_pairs={{4,0},{8,4},{12,8},{16,12},{20,16},{24,20},{28,24},{5,1},{9,5},{13... | collective-permute-start | bytes 786440 | tf_op jit(solution)/shard_map/ppermute | solution.py:29
  90.1 2.7 %collective-permute-start.6 = (f32[2,34,1,512]{3,2,1,0:T(1,128)S(1)}, f32[2,34,1,512]{3,2,1,0:T(1,128)S(1)}, u32[]{:S(2)}, u32[]{:S(2)}) collective-permute-start(f32[2,34,1,512]{3,2,1,0:T(1,128)S(1)} %get-tuple-element.16), channel_id=1, source_target_pairs={{0,1},{1,2},{2,3},{4,5},{5,6},{6,7},{8,9},{9,10},{10,11},{12,13},{... | collective-permute-start | bytes 417800 | tf_op jit(solution)/shard_map/ppermute | solution.py:27
  92.7 3.4 %collective-permute-start.7 = (f32[2,34,1,512]{3,2,1,0:T(1,128)S(1)}, f32[2,34,1,512]{3,2,1,0:T(1,128)S(1)}, u32[]{:S(2)}, u32[]{:S(2)}) collective-permute-start(f32[2,34,1,512]{3,2,1,0:T(1,128)S(1)} %get-tuple-element.17), channel_id=1, source_target_pairs={{1,0},{2,1},{3,2},{5,4},{6,5},{7,6},{9,8},{10,9},{11,10},{13,12},{... | collective-permute-start | bytes 417800 | tf_op jit(solution)/shard_map/ppermute | solution.py:29
  99.9 8.6 %pad_maximum_fusion.1 = f32[2,34,66,512]{3,2,1,0:T(8,128)} fusion(f32[2,34,1,512]{3,2,1,0:T(1,128)S(1)} %collective-permute-done.7, f32[2,1,64,512]{3,2,1,0:T(8,128)S(1)} %collective-permute-done.5, f32[1,32,64,512]{3,2,1,0:T(8,128)S(1)} %copy-done.2, f32[1,32,64,512]{3,2,1,0:T(8,128)S(1)} %copy-done, f32[2,1,64,512]{3,2,1,0:T(8,128)S(1)} %collective-permute-done.4, ...), kind=kLoop, calls=%fused_computation.3 | loop fusion | flops 11489280 | bytes 18382848 | tf_op jit(solution)/shard_map/concatenate | solution.py:25
  108.6 7.5 %slice_bitcast_fusion.3 = (f32[34,66,512]{2,1,0:T(8,128)}, f32[34,66,512]{2,1,0:T(8,128)S(1)}) fusion(f32[2,34,66,512]{3,2,1,0:T(8,128)} %pad_maximum_fusion.1), kind=kLoop, calls=%fused_computation.29 | loop fusion | bytes 18382848 | tf_op jit(solution)/shard_map/squeeze | solution.py:113
  116.9 21.2 %add_bitcast_fusion = (f32[1,32,64,512]{3,2,1,0:T(8,128)}, f32[32,64,512]{2,1,0:T(8,128)}) fusion(f32[34,66,512]{2,1,0:T(8,128)} %get-tuple-element.10, f32[34,66,512]{2,1,0:T(8,128)S(1)} %get-tuple-element.11, f32[32,8,512]{2,1,0:T(8,128)} %bitcast.78, f32[32,64]{1,0:T(8,128)S(1)} %copy.13), kind=kLoop, calls=%fused_computation.122 | loop fusion | flops 26214400 | bytes 39100416 | tf_op jit(solution)/shard_map/stack | solution.py:112
  138.1 9.3 %fusion.37 = f32[1,32,64,512]{3,2,1,0:T(8,128)} fusion(f32[34,66,512]{2,1,0:T(8,128)S(1)} %get-tuple-element.11, f32[32,64,512]{2,1,0:T(8,128)} %get-tuple-element.5), kind=kLoop, calls=%fused_computation.69 | loop fusion | flops 14680064 | bytes 34373632 | tf_op jit(solution)/shard_map/stack | solution.py:112
  150.6 4.5 %collective-permute-start.9 = (f32[2,1,64,512]{3,2,1,0:T(8,128)S(1)}, f32[2,1,64,512]{3,2,1,0:T(8,128)S(1)}, u32[]{:S(2)}, u32[]{:S(2)}) collective-permute-start(f32[2,1,64,512]{3,2,1,0:T(8,128)S(1)} %get-tuple-element.21), channel_id=1, source_target_pairs={{4,0},{8,4},{12,8},{16,12},{20,16},{24,20},{28,24},{5,1},{9,5},{13... | collective-permute-start | bytes 786440 | tf_op jit(solution)/shard_map/ppermute | solution.py:29
  155.2 3.1 %collective-permute-done.8 = f32[2,1,64,512]{3,2,1,0:T(8,128)S(1)} collective-permute-done((f32[2,1,64,512]{3,2,1,0:T(8,128)S(1)}, f32[2,1,64,512]{3,2,1,0:T(8,128)S(1)}, u32[]{:S(2)}, u32[]{:S(2)}) %collective-permute-start.8) | collective-permute-done | bytes 262176 | tf_op jit(solution)/shard_map/ppermute | solution.py:27
  159.3 3.4 %collective-permute-start.10 = (f32[2,34,1,512]{3,2,1,0:T(1,128)S(1)}, f32[2,34,1,512]{3,2,1,0:T(1,128)S(1)}, u32[]{:S(2)}, u32[]{:S(2)}) collective-permute-start(f32[2,34,1,512]{3,2,1,0:T(1,128)S(1)} %get-tuple-element.14), channel_id=1, source_target_pairs={{0,1},{1,2},{2,3},{4,5},{5,6},{6,7},{8,9},{9,10},{10,11},{12,13},{... | collective-permute-start | bytes 417800 | tf_op jit(solution)/shard_map/ppermute | solution.py:27
  162.7 2.7 %collective-permute-start.11 = (f32[2,34,1,512]{3,2,1,0:T(1,128)S(1)}, f32[2,34,1,512]{3,2,1,0:T(1,128)S(1)}, u32[]{:S(2)}, u32[]{:S(2)}) collective-permute-start(f32[2,34,1,512]{3,2,1,0:T(1,128)S(1)} %get-tuple-element.15), channel_id=1, source_target_pairs={{1,0},{2,1},{3,2},{5,4},{6,5},{7,6},{9,8},{10,9},{11,10},{13,12},{... | collective-permute-start | bytes 417800 | tf_op jit(solution)/shard_map/ppermute | solution.py:29
  166.3 3.4 %collective-permute-done.11 = f32[2,34,1,512]{3,2,1,0:T(1,128)S(1)} collective-permute-done((f32[2,34,1,512]{3,2,1,0:T(1,128)S(1)}, f32[2,34,1,512]{3,2,1,0:T(1,128)S(1)}, u32[]{:S(2)}, u32[]{:S(2)}) %collective-permute-start.11) | collective-permute-done | bytes 139296 | tf_op jit(solution)/shard_map/ppermute | solution.py:29
  169.7 8.6 %pad_maximum_fusion.2 = f32[2,34,66,512]{3,2,1,0:T(8,128)} fusion(f32[2,34,1,512]{3,2,1,0:T(1,128)S(1)} %collective-permute-done.11, f32[2,1,64,512]{3,2,1,0:T(8,128)S(1)} %collective-permute-done.9, f32[1,32,64,512]{3,2,1,0:T(8,128)S(1)} %copy-done.3, f32[1,32,64,512]{3,2,1,0:T(8,128)S(1)} %copy-done.1, f32[2,1,64,512]{3,2,1,0:T(8,128)S(1)} %collective-permute-done.8, ...), kind=kLoop, calls=%fused_computation.4 | loop fusion | flops 11489280 | bytes 18382848 | tf_op jit(solution)/shard_map/concatenate | solution.py:25
  178.3 5.1 %slice_bitcast_fusion.1 = (f32[34,66,512]{2,1,0:T(8,128)S(1)}, f32[34,66,512]{2,1,0:T(8,128)S(1)}) fusion(f32[2,34,66,512]{3,2,1,0:T(8,128)} %pad_maximum_fusion.2), kind=kLoop, calls=%fused_computation.27 | loop fusion | bytes 18382848 | tf_op jit(solution)/shard_map/squeeze | solution.py:113
  183.4 15.1 %fusion.49 = (f32[32,64,512]{2,1,0:T(8,128)}, f32[32,64,512]{2,1,0:T(8,128)S(1)}) fusion(f32[34,66,512]{2,1,0:T(8,128)S(1)} %get-tuple-element.9, f32[32,8,512]{2,1,0:T(8,128)S(1)} %bitcast.76, f32[34,66,512]{2,1,0:T(8,128)S(1)} %get-tuple-element.8, f32[32,64]{1,0:T(8,128)S(1)} %copy.13), kind=kLoop, calls=%fused_computation.81 | loop fusion | flops 38797312 | bytes 60899328 | tf_op jit(solution)/shard_map/add | solution.py:58
  198.6 3.1 %multiply_add_fusion = f32[32,64,512]{2,1,0:T(8,128)} fusion(f32[32,64,512]{2,1,0:T(8,128)S(1)} %get-tuple-element.3, f32[34,66,512]{2,1,0:T(8,128)S(1)} %get-tuple-element.8), kind=kLoop, calls=%fused_computation.121 | loop fusion | flops 2097152 | bytes 12582912 | tf_op jit(solution)/shard_map/add | solution.py:57
  (70 shorter events, 34.3 us)
Async XLA Ops:
  0.6 7.6 %copy-start.7 = (s32[64,1]{0,1:T(1,128)S(1)}, s32[64,1]{0,1:T(1,128)}, u32[]{:S(2)}) copy-start(s32[64,1]{0,1:T(1,128)} %param.11) | copy-start | bytes 772
  0.6 14.7 %copy-start.8 = (s32[4,8]{1,0:T(4,128)S(1)}, s32[4,8]{1,0:T(4,128)}, u32[]{:S(2)}) copy-start(s32[4,8]{1,0:T(4,128)} %param.13) | copy-start | bytes 388
  1.8 13.8 %collective-permute-start = (f32[2,1,64,512]{3,2,1,0:T(8,128)S(1)}, f32[2,1,64,512]{3,2,1,0:T(8,128)S(1)}, u32[]{:S(2)}, u32[]{:S(2)}) collective-permute-start(f32[2,1,64,512]{3,2,1,0:T(8,128)S(1)} %get-tuple-element.24), channel_id=1, source_target_pairs={{0,4},{4,8},{8,12},{12,16},{16,20},{20,24},{24,28},{1,5},{5,9},{9,... | collective-permute-start | bytes 786440 | tf_op jit(solution)/shard_map/ppermute | solution.py:27
  3.7 11.9 %collective-permute-start.1 = (f32[2,1,64,512]{3,2,1,0:T(8,128)S(1)}, f32[2,1,64,512]{3,2,1,0:T(8,128)S(1)}, u32[]{:S(2)}, u32[]{:S(2)}) collective-permute-start(f32[2,1,64,512]{3,2,1,0:T(8,128)S(1)} %get-tuple-element.25), channel_id=1, source_target_pairs={{4,0},{8,4},{12,8},{16,12},{20,16},{24,20},{28,24},{5,1},{9,5},{13... | collective-permute-start | bytes 786440 | tf_op jit(solution)/shard_map/ppermute | solution.py:29
  10.3 15.1 %all-to-all-start = ((s32[32,1,4]{2,1,0:T(1,128)}), s32[32,1,4]{2,1,0:T(1,128)S(1)}, u32[]{:S(2)}, u32[]{:S(2)}) async-start(s32[32,1,4]{2,1,0:T(1,128)} %bitcast.7), calls=%async_computation | async-start | bytes 32768 | tf_op jit(solution)/shard_map/all_to_all | solution.py:91
  15.6 7.7 %copy-start.5 = (f32[64,512]{1,0:T(8,128)S(1)}, f32[64,512]{1,0:T(8,128)}, u32[]{:S(2)}) copy-start(f32[64,512]{1,0:T(8,128)} %param.10) | copy-start | bytes 393220
  15.6 7.7 %copy-start.6 = (f32[64,512]{1,0:T(8,128)S(1)}, f32[64,512]{1,0:T(8,128)}, u32[]{:S(2)}) copy-start(f32[64,512]{1,0:T(8,128)} %param.9) | copy-start | bytes 393220
  17.5 15.0 %collective-permute-start.2 = (f32[2,34,1,512]{3,2,1,0:T(1,128)S(1)}, f32[2,34,1,512]{3,2,1,0:T(1,128)S(1)}, u32[]{:S(2)}, u32[]{:S(2)}) collective-permute-start(f32[2,34,1,512]{3,2,1,0:T(1,128)S(1)} %get-tuple-element.18), channel_id=1, source_target_pairs={{0,1},{1,2},{2,3},{4,5},{5,6},{6,7},{8,9},{9,10},{10,11},{12,13},{... | collective-permute-start | bytes 417800 | tf_op jit(solution)/shard_map/ppermute | solution.py:27
  20.9 11.7 %collective-permute-start.3 = (f32[2,34,1,512]{3,2,1,0:T(1,128)S(1)}, f32[2,34,1,512]{3,2,1,0:T(1,128)S(1)}, u32[]{:S(2)}, u32[]{:S(2)}) collective-permute-start(f32[2,34,1,512]{3,2,1,0:T(1,128)S(1)} %get-tuple-element.19), channel_id=1, source_target_pairs={{1,0},{2,1},{3,2},{5,4},{6,5},{7,6},{9,8},{10,9},{11,10},{13,12},{... | collective-permute-start | bytes 417800 | tf_op jit(solution)/shard_map/ppermute | solution.py:29
  25.4 20.1 %all-to-all-start.1 = ((f32[32,4,1024]{2,1,0:T(4,128)}), f32[32,4,1024]{2,1,0:T(4,128)S(1)}, u32[]{:S(2)}, u32[]{:S(2)}) async-start(f32[32,4,1024]{2,1,0:T(4,128)} %reshape.73), calls=%async_computation.1 | async-start | bytes 1048576 | tf_op jit(solution)/shard_map/all_to_all | solution.py:84
  46.9 22.0 %slice-start = ((s8[5013504]{0:T(1024)(128)(4,1)}), s8[4194304]{0:T(1024)(128)(4,1)S(1)}, s32[]{:S(2)}) async-start(s8[5013504]{0:T(1024)(128)(4,1)} %bitcast.68), calls=%async_computation.2 | async-start | bytes 8388608
  47.7 21.1 %slice-start.1 = ((s8[5013504]{0:T(1024)(128)(4,1)}), s8[819200]{0:T(1024)(128)(4,1)S(1)}, s32[]{:S(2)}) async-start(s8[5013504]{0:T(1024)(128)(4,1)} %bitcast.68), calls=%async_computation.3 | async-start | bytes 1638400
  68.8 9.3 %copy-start = (f32[1,32,64,512]{3,2,1,0:T(8,128)S(1)}, f32[1,32,64,512]{3,2,1,0:T(8,128)}, u32[]{:S(2)}) copy-start(f32[1,32,64,512]{3,2,1,0:T(8,128)} %get-tuple-element.6) | copy-start | bytes 12582916
  78.2 11.6 %copy-start.2 = (f32[1,32,64,512]{3,2,1,0:T(8,128)S(1)}, f32[1,32,64,512]{3,2,1,0:T(8,128)}, u32[]{:S(2)}) copy-start(f32[1,32,64,512]{3,2,1,0:T(8,128)} %fusion.24) | copy-start | bytes 12582916
  79.3 9.1 %collective-permute-start.4 = (f32[2,1,64,512]{3,2,1,0:T(8,128)S(1)}, f32[2,1,64,512]{3,2,1,0:T(8,128)S(1)}, u32[]{:S(2)}, u32[]{:S(2)}) collective-permute-start(f32[2,1,64,512]{3,2,1,0:T(8,128)S(1)} %get-tuple-element.22), channel_id=1, source_target_pairs={{0,4},{4,8},{8,12},{12,16},{16,20},{20,24},{24,28},{1,5},{5,9},{9,... | collective-permute-start | bytes 786440 | tf_op jit(solution)/shard_map/ppermute | solution.py:27
  81.4 8.4 %collective-permute-start.5 = (f32[2,1,64,512]{3,2,1,0:T(8,128)S(1)}, f32[2,1,64,512]{3,2,1,0:T(8,128)S(1)}, u32[]{:S(2)}, u32[]{:S(2)}) collective-permute-start(f32[2,1,64,512]{3,2,1,0:T(8,128)S(1)} %get-tuple-element.23), channel_id=1, source_target_pairs={{4,0},{8,4},{12,8},{16,12},{20,16},{24,20},{28,24},{5,1},{9,5},{13... | collective-permute-start | bytes 786440 | tf_op jit(solution)/shard_map/ppermute | solution.py:29
  90.1 7.6 %collective-permute-start.6 = (f32[2,34,1,512]{3,2,1,0:T(1,128)S(1)}, f32[2,34,1,512]{3,2,1,0:T(1,128)S(1)}, u32[]{:S(2)}, u32[]{:S(2)}) collective-permute-start(f32[2,34,1,512]{3,2,1,0:T(1,128)S(1)} %get-tuple-element.16), channel_id=1, source_target_pairs={{0,1},{1,2},{2,3},{4,5},{5,6},{6,7},{8,9},{9,10},{10,11},{12,13},{... | collective-permute-start | bytes 417800 | tf_op jit(solution)/shard_map/ppermute | solution.py:27
  92.7 7.2 %collective-permute-start.7 = (f32[2,34,1,512]{3,2,1,0:T(1,128)S(1)}, f32[2,34,1,512]{3,2,1,0:T(1,128)S(1)}, u32[]{:S(2)}, u32[]{:S(2)}) collective-permute-start(f32[2,34,1,512]{3,2,1,0:T(1,128)S(1)} %get-tuple-element.17), channel_id=1, source_target_pairs={{1,0},{2,1},{3,2},{5,4},{6,5},{7,6},{9,8},{10,9},{11,10},{13,12},{... | collective-permute-start | bytes 417800 | tf_op jit(solution)/shard_map/ppermute | solution.py:29
  138.1 9.3 %copy-start.1 = (f32[1,32,64,512]{3,2,1,0:T(8,128)S(1)}, f32[1,32,64,512]{3,2,1,0:T(8,128)}, u32[]{:S(2)}) copy-start(f32[1,32,64,512]{3,2,1,0:T(8,128)} %get-tuple-element.4) | copy-start | bytes 12582916
  147.4 11.6 %copy-start.3 = (f32[1,32,64,512]{3,2,1,0:T(8,128)S(1)}, f32[1,32,64,512]{3,2,1,0:T(8,128)}, u32[]{:S(2)}) copy-start(f32[1,32,64,512]{3,2,1,0:T(8,128)} %fusion.37) | copy-start | bytes 12582916
  148.6 9.7 %collective-permute-start.8 = (f32[2,1,64,512]{3,2,1,0:T(8,128)S(1)}, f32[2,1,64,512]{3,2,1,0:T(8,128)S(1)}, u32[]{:S(2)}, u32[]{:S(2)}) collective-permute-start(f32[2,1,64,512]{3,2,1,0:T(8,128)S(1)} %get-tuple-element.20), channel_id=1, source_target_pairs={{0,4},{4,8},{8,12},{12,16},{16,20},{20,24},{24,28},{1,5},{5,9},{9,... | collective-permute-start | bytes 786440 | tf_op jit(solution)/shard_map/ppermute | solution.py:27
  150.6 8.4 %collective-permute-start.9 = (f32[2,1,64,512]{3,2,1,0:T(8,128)S(1)}, f32[2,1,64,512]{3,2,1,0:T(8,128)S(1)}, u32[]{:S(2)}, u32[]{:S(2)}) collective-permute-start(f32[2,1,64,512]{3,2,1,0:T(8,128)S(1)} %get-tuple-element.21), channel_id=1, source_target_pairs={{4,0},{8,4},{12,8},{16,12},{20,16},{24,20},{28,24},{5,1},{9,5},{13... | collective-permute-start | bytes 786440 | tf_op jit(solution)/shard_map/ppermute | solution.py:29
  159.3 6.9 %collective-permute-start.10 = (f32[2,34,1,512]{3,2,1,0:T(1,128)S(1)}, f32[2,34,1,512]{3,2,1,0:T(1,128)S(1)}, u32[]{:S(2)}, u32[]{:S(2)}) collective-permute-start(f32[2,34,1,512]{3,2,1,0:T(1,128)S(1)} %get-tuple-element.14), channel_id=1, source_target_pairs={{0,1},{1,2},{2,3},{4,5},{5,6},{6,7},{8,9},{9,10},{10,11},{12,13},{... | collective-permute-start | bytes 417800 | tf_op jit(solution)/shard_map/ppermute | solution.py:27
  162.7 6.9 %collective-permute-start.11 = (f32[2,34,1,512]{3,2,1,0:T(1,128)S(1)}, f32[2,34,1,512]{3,2,1,0:T(1,128)S(1)}, u32[]{:S(2)}, u32[]{:S(2)}) collective-permute-start(f32[2,34,1,512]{3,2,1,0:T(1,128)S(1)} %get-tuple-element.15), channel_id=1, source_target_pairs={{1,0},{2,1},{3,2},{5,4},{6,5},{7,6},{9,8},{10,9},{11,10},{13,12},{... | collective-permute-start | bytes 417800 | tf_op jit(solution)/shard_map/ppermute | solution.py:29
  (1 other events, 7.5 us)
where the time goes:
time: 203 us; the launch traced here: 202 us
  other arithmetic  111 us (55%)
  starting transfers between devices  48.5 us (24%)
  local copies, waits for them, and re-layouts  23.2 us (11%)
  waiting for transfers between devices  17.7 us (9%)
    another operation x4, other arithmetic, on_device(): jnp.stack([phase, solute])  60.9 us
    concatenate x3, other arithmetic, extended_2(): jnp.concatenate([lax.ppermute(tail, axis, [(i, (i + 1) % count) for i in...  23.2 us
    ppermute x6, starting transfers between devices, extended_2(): lax.ppermute(head, axis, [((i + 1) % count, i) for i in range(ends)])  22.1 us
    squeeze x3, local copies, waits for them, and re-layouts, on_device(): phase, solute = advance(extended[0], extended[1], heat, rate, cells, count)  17.5 us
    ppermute x6, starting transfers between devices, extended_2(): lax.ppermute(tail, axis, [(i, (i + 1) % count) for i in range(ends)])  15.4 us
    add x1, other arithmetic, advance(): inner_solute + time_step * (diffusion * laplace(solute_ext, 1.0, 1.0, 1.0...  15.1 us
    ppermute x6, waiting for transfers between devices, extended_2(): lax.ppermute(tail, axis, [(i, (i + 1) % count) for i in range(ends)])  8.03 us
    ppermute x6, waiting for transfers between devices, extended_2(): lax.ppermute(head, axis, [((i + 1) % count, i) for i in range(ends)])  7.8 us
  transfers between devices with their start and end apart: 14, of which 9 were waited for; matrix products, arithmetic and copies ran while one was open for 9% of the time, Pallas kernels for 0%

commit v1 on v0

v1 whole, which is shorter than its diff:
```python
import functools

import jax
import jax.numpy as jnp
from jax import lax
from jax.experimental import pallas as pl
from jax.experimental.pallas import tpu as pltpu
from jax.sharding import PartitionSpec as P

BS = 8
CAP = 4
STEPS = 3
LANES = 128
PAD = 8
MESH = pl.DeviceIdType.MESH
HIGH = lax.Precision.HIGHEST

coef_track = 0.9
coef_width = 0.6
coef_depth = 0.35
time_step = 0.1
coupling = 1.6
diffusion = 0.8
center_phase = 1.0 - 2.0 * (coef_track + coef_width + coef_depth)
center_solute = 1.0 - 6.0 * time_step * diffusion


def track_kernel(sizes, phase, solute, heat_rows, rate_rows, dest_tile, dest_block, active,
                 phase_out, solute_out,
                 f0, f1, y_send, y_recv, label_out, label_in, heat_out, heat_in, rate_out, rate_in,
                 selector, theta,
                 load_sem, store_sem, x_send_sem, x_recv_sem, y_send_sem, y_recv_sem,
                 label_sems, heat_sems, rate_sems):
    tracks, widths, nx, ny, nz, rows = sizes
    devices = tracks * widths
    zt_n = nz // LANES
    pairs = zt_n // 2
    bx_n = nx // BS
    by_n = ny // BS
    t = lax.axis_index("track")
    w = lax.axis_index("width")
    me = t * widths + w

    def loads():
        out = []
        for f, ref in enumerate((phase, solute)):
            for zt in range(zt_n):
                out.append(pltpu.make_async_copy(
                    ref.at[:, :, pl.ds(zt * LANES, LANES)],
                    f0.at[f, pl.ds(1, nx), zt, pl.ds(PAD, ny), :],
                    load_sem.at[f, zt]))
        return out

    for copy in loads():
        copy.start()

    barrier = pltpu.get_barrier_semaphore()

    def where(k):
        to = lax.rem(me + k, devices)
        return {"track": to // widths, "width": lax.rem(to, widths)}

    def greet(k, carry):
        pl.semaphore_signal(barrier, inc=1, device_id=where(k), device_id_type=MESH)
        return carry

    lax.fori_loop(1, devices, greet, 0)

    tcol = dest_tile[...].astype(jnp.float32)
    eye = lax.broadcasted_iota(jnp.int32, (rows, rows), 0) == lax.broadcasted_iota(jnp.int32, (rows, rows), 1)
    trow = jnp.sum(jnp.where(eye, tcol, 0.0), axis=0, keepdims=True)
    before = lax.broadcasted_iota(jnp.int32, (rows, rows), 0) < lax.broadcasted_iota(jnp.int32, (rows, rows), 1)
    rank = jnp.sum(jnp.where(before & (tcol == trow), 1.0, 0.0), axis=0, keepdims=True)
    slot = trow * CAP + rank
    index = lax.broadcasted_iota(jnp.int32, (8 * devices, rows), 0)
    slot_of = ((index >> 3) * CAP + (index & 3)).astype(jnp.float32)
    pick = jnp.where(slot_of == slot, 1.0, 0.0)
    labels = dest_block[...].astype(jnp.float32) + 1.0
    label_col = jnp.sum(pick * labels, axis=1, keepdims=True).reshape(devices, 8, 1)
    diagonal = lax.broadcasted_iota(jnp.int32, (devices, 8, LANES), 1) == lax.broadcasted_iota(
        jnp.int32, (devices, 8, LANES), 2)
    label_out[...] = jnp.sum(jnp.where(diagonal, label_col, 0.0), axis=1, keepdims=True)
    low = lax.broadcasted_iota(jnp.int32, (8 * devices, LANES), 0) & 7 < 4

    def pack_rows(source, target):
        moved = jnp.dot(pick, source[...], precision=HIGH, preferred_element_type=jnp.float32)
        for j in range(pairs):
            first = moved[:, 2 * j * LANES:(2 * j + 1) * LANES]
            second = moved[:, (2 * j + 1) * LANES:(2 * j + 2) * LANES]
            target[:, j] = jnp.where(low, first, second).reshape(devices, 8, LANES)

    pack_rows(heat_rows, heat_out)
    pack_rows(rate_rows, rate_out)

    has = (t > 0, t < tracks - 1, w > 0, w < widths - 1)
    for side in range(2):
        @pl.when(jnp.logical_not(has[side]))
        def _():
            edge = jnp.zeros((2, zt_n, ny, LANES), jnp.float32)
            f0[:, side * (nx + 1), :, pl.ds(PAD, ny), :] = edge
            f1[:, side * (nx + 1), :, pl.ds(PAD, ny), :] = edge

        @pl.when(jnp.logical_not(has[2 + side]))
        def _():
            y_recv[:, side] = jnp.zeros((STEPS, 2, nx, zt_n, 1, LANES), jnp.float32)

    pl.semaphore_wait(barrier, devices - 1)

    def exchange(source, target, sems, k):
        return pltpu.make_async_remote_copy(
            src_ref=source.at[lax.rem(me + k, devices)], dst_ref=target.at[me],
            send_sem=sems.at[0, k], recv_sem=sems.at[1, k],
            device_id=where(k), device_id_type=MESH)

    def own(source, target, sems):
        return pltpu.make_async_copy(source.at[me], target.at[me], sems.at[0, 0])

    def send_all(*triples):
        for triple in triples:
            own(*triple).start()

        def body(k, carry):
            for triple in triples:
                exchange(*triple, k).start()
            return carry

        lax.fori_loop(1, devices, body, 0)

    def wait_all(*triples):
        for triple in triples:
            own(*triple).wait()

        def body(k, carry):
            for triple in triples:
                exchange(*triple, k).wait()
            return carry

        lax.fori_loop(1, devices, body, 0)

    labels_x = (label_out, label_in, label_sems)
    heat_x = (heat_out, heat_in, heat_sems)
    rate_x = (rate_out, rate_in, rate_sems)
    send_all(labels_x, heat_x)

    def x_copy(field, stage, side):
        return pltpu.make_async_remote_copy(
            src_ref=field.at[:, 1 if side == 0 else nx, :, pl.ds(PAD, ny), :],
            dst_ref=field.at[:, nx + 1 if side == 0 else 0, :, pl.ds(PAD, ny), :],
            send_sem=x_send_sem.at[stage, side], recv_sem=x_recv_sem.at[stage, side],
            device_id={"track": t + (2 * side - 1)}, device_id_type=MESH)

    def y_copy(stage, side):
        return pltpu.make_async_remote_copy(
            src_ref=y_send.at[stage, side], dst_ref=y_recv.at[stage, 1 - side],
            send_sem=y_send_sem.at[stage, side], recv_sem=y_recv_sem.at[stage, side],
            device_id={"width": w + (2 * side - 1)}, device_id_type=MESH)

    def send_halo(field, stage):
        for side in range(2):
            @pl.when(has[side])
            def _():
                x_copy(field, stage, side).start()

        def pack(x, carry):
            for side, row in ((0, PAD), (1, PAD + ny - 1)):
                for f in range(2):
                    for zt in range(zt_n):
                        y_send[stage, side, f, x, zt] = field[f, x + 1, zt, pl.ds(row, 1), :]
            return carry

        lax.fori_loop(0, nx, pack, 0)
        for side in range(2):
            @pl.when(has[2 + side])
            def _():
                y_copy(stage, side).start()

    def wait_halo(field, stage):
        for side in range(2):
            @pl.when(has[side])
            def _():
                x_copy(field, stage, side).wait_send()
                x_copy(field, stage, 1 - side).wait_recv()

            @pl.when(has[2 + side])
            def _():
                y_copy(stage, side).wait_send()
                y_copy(stage, 1 - side).wait_recv()

        def unpack(x, carry):
            for side, row in ((0, PAD - 1), (1, PAD + ny)):
                for f in range(2):
                    for zt in range(zt_n):
                        field[f, x + 1, zt, pl.ds(row, 1), :] = y_recv[stage, side, f, x, zt]
            return carry

        lax.fori_loop(0, nx, unpack, 0)

    lane = lax.broadcasted_iota(jnp.int32, (BS, LANES), 1)
    first_lane = lane == 0
    last_lane = lane == LANES - 1

    def depth_sum(tiles):
        up = [pltpu.roll(v, 1, 1) for v in tiles]
        down = [pltpu.roll(v, LANES - 1, 1) for v in tiles]
        sums = []
        for zt in range(zt_n):
            below = jnp.where(first_lane, up[zt - 1] if zt > 0 else 0.0, up[zt])
            above = jnp.where(last_lane, down[zt + 1] if zt < zt_n - 1 else 0.0, down[zt])
            sums.append(below + above)
        return sums

    def cell_block(src, dst, count, x, by):
        bx = x >> 3
        rate_of = active[bx, by].astype(jnp.float32) * time_step
        here = pl.ds(PAD + BS * by, BS)
        back = pl.ds(PAD + BS * by - 1, BS)
        ahead = pl.ds(PAD + BS * by + 1, BS)
        p = [src[0, x + 1, zt, here, :] for zt in range(zt_n)]
        s = [src[1, x + 1, zt, here, :] for zt in range(zt_n)]
        pz = depth_sum(p)
        sz = depth_sum(s)
        for zt in range(zt_n):
            px = src[0, x, zt, here, :] + src[0, x + 2, zt, here, :]
            py = src[0, x + 1, zt, back, :] + src[0, x + 1, zt, ahead, :]
            sx = src[1, x, zt, here, :] + src[1, x + 2, zt, here, :]
            sy = src[1, x + 1, zt, back, :] + src[1, x + 1, zt, ahead, :]
            square = p[zt] * p[zt]
            bond = 1.0 - square
            drive = coef_track * px + coef_width * py + coef_depth * pz[zt] + p[zt] * (center_phase - square)
            sink = s[zt] if count == 0 else s[zt] + theta[count - 1, bx, zt, by:by + 1, :]
            drive = drive - coupling * bond * bond * sink
            change = rate_of * drive
            dst[0, x + 1, zt, here, :] = p[zt] + change
            dst[1, x + 1, zt, here, :] = (
                center_solute * s[zt] + (time_step * diffusion) * (sx + sy + sz[zt]) + 0.5 * change)

    def heat_block(src, dst, x, by):
        bx = x >> 3
        rate_of = active[bx, by].astype(jnp.float32) * (time_step * coupling)
        here = pl.ds(PAD + BS * by, BS)
        for zt in range(zt_n):
            p = src[0, x + 1, zt, here, :]
            bond = 1.0 - p * p
            change = bond * bond * (rate_of * theta[0, bx, zt, by:by + 1, :])
            dst[0, x + 1, zt, here, :] = dst[0, x + 1, zt, here, :] - change
            dst[1, x + 1, zt, here, :] = dst[1, x + 1, zt, here, :] - 0.5 * change

    def sweep(block, xs, bys):
        low_x, high_x, stride = xs

        def body(i, carry):
            for by in bys:
                block(low_x + stride * i, by)
            return carry

        lax.fori_loop(0, (high_x - low_x + stride - 1) // stride, body, 0)

    inner = range(1, by_n - 1)
    outer = (0, by_n - 1)

    def boundary(block):
        sweep(block, (0, nx, nx - 1), range(by_n))
        sweep(block, (1, nx - 1, 1), outer)

    def arrived(rows_in):
        both = jnp.concatenate([rows_in[:, j].reshape(8 * devices, LANES) for j in range(pairs)], axis=1)
        return lax.dot_general(selector[...], both, (((0,), (0,)), ((), ())), precision=HIGH,
                               preferred_element_type=jnp.float32)

    def tile_of(summed, bx, zt):
        at = (zt % 2) * (LANES // 2) + bx * by_n
        return summed[at:at + by_n, (zt // 2) * LANES:(zt // 2 + 1) * LANES]

    for copy in loads():
        copy.wait()
    send_halo(f0, 0)
    send_all(rate_x)

    step0 = functools.partial(cell_block, f0, f1, 0)
    step1 = functools.partial(cell_block, f1, f0, 1)
    step2 = functools.partial(cell_block, f0, f1, 2)
    finish = functools.partial(heat_block, f0, f1)

    sweep(step0, (1, nx - 1, 1), inner)
    wait_halo(f0, 0)
    boundary(step0)

    wait_all(labels_x, heat_x)
    spread = jnp.where(diagonal, jnp.broadcast_to(label_in[...], (devices, 8, LANES)), 0.0)
    label_in_col = jnp.sum(spread, axis=2, keepdims=True) - 1.0
    place = lax.broadcasted_iota(jnp.int32, (devices, 8, LANES), 2) - (LANES // 2) * (
        lax.broadcasted_iota(jnp.int32, (devices, 8, LANES), 1) >> 2)
    selector[...] = jnp.where(place.astype(jnp.float32) == label_in_col, 1.0, 0.0).reshape(8 * devices, LANES)
    heat = arrived(heat_in)
    for bx in range(bx_n):
        for zt in range(zt_n):
            theta[0, bx, zt] = tile_of(heat, bx, zt)

    boundary(finish)
    send_halo(f1, 1)
    sweep(finish, (1, nx - 1, 1), inner)

    wait_all(rate_x)
    rate = arrived(rate_in)
    for bx in range(bx_n):
        for zt in range(zt_n):
            whole = theta[0, bx, zt]
            slope = tile_of(rate, bx, zt)
            theta[0, bx, zt] = whole - time_step * slope
            theta[1, bx, zt] = whole - (2 * time_step) * slope

    half = nx // 2
    sweep(step1, (1, half, 1), inner)
    wait_halo(f1, 1)
    boundary(step1)
    send_halo(f0, 2)
    sweep(step1, (half, nx - 1, 1), inner)
    sweep(step2, (1, nx - 1, 1), inner)

    def stores(part, x_at, x_len, y_at, y_len):
        out = []
        for f, ref in enumerate((phase_out, solute_out)):
            for zt in range(zt_n):
                out.append(pltpu.make_async_copy(
                    f1.at[f, pl.ds(1 + x_at, x_len), zt, pl.ds(PAD + y_at, y_len), :],
                    ref.at[pl.ds(x_at, x_len), pl.ds(y_at, y_len), pl.ds(zt * LANES, LANES)],
                    store_sem.at[part, f, zt]))
        return out

    middle = stores(0, 1, nx - 2, BS, ny - 2 * BS)
    for copy in middle:
        copy.start()
    wait_halo(f0, 2)
    boundary(step2)
    rim = (stores(1, 0, 1, 0, ny) + stores(2, nx - 1, 1, 0, ny)
           + stores(3, 1, nx - 2, 0, BS) + stores(4, 1, nx - 2, ny - BS, BS))
    for copy in rim:
        copy.start()
    for copy in middle + rim:
        copy.wait()


def solution(mesh):
    tracks = mesh.shape["track"]
    widths = mesh.shape["width"]
    devices = tracks * widths

    def on_device(phase, solute, heat_rows, rate_rows, dest_tile, dest_block, active):
        nx, ny, nz = phase.shape
        rows = heat_rows.shape[0]
        zt_n = nz // LANES
        pairs = zt_n // 2
        f32 = jnp.float32
        field = pltpu.VMEM((2, nx + 2, zt_n, ny + 2 * PAD, LANES), f32)
        ends = pltpu.VMEM((STEPS, 2, 2, nx, zt_n, 1, LANES), f32)
        label = pltpu.VMEM((devices, 1, LANES), f32)
        moved = pltpu.VMEM((devices, pairs, 8, LANES), f32)
        vmem = pl.BlockSpec(memory_space=pltpu.VMEM)
        any_space = pl.BlockSpec(memory_space=pl.ANY)
        return pl.pallas_call(
            functools.partial(track_kernel, (tracks, widths, nx, ny, nz, rows)),
            out_shape=(jax.ShapeDtypeStruct(phase.shape, f32), jax.ShapeDtypeStruct(solute.shape, f32)),
            in_specs=[any_space, any_space, vmem, vmem, vmem, vmem,
                      pl.BlockSpec(memory_space=pltpu.SMEM)],
            out_specs=(any_space, any_space),
            scratch_shapes=[
                field, field, ends, ends, label, label, moved, moved, moved, moved,
                pltpu.VMEM((8 * devices, LANES), f32),
                pltpu.VMEM((2, nx // BS, zt_n, ny // BS, LANES), f32),
                pltpu.SemaphoreType.DMA((2, zt_n)),
                pltpu.SemaphoreType.DMA((5, 2, zt_n)),
                pltpu.SemaphoreType.DMA((STEPS, 2)),
                pltpu.SemaphoreType.DMA((STEPS, 2)),
                pltpu.SemaphoreType.DMA((STEPS, 2)),
                pltpu.SemaphoreType.DMA((STEPS, 2)),
                pltpu.SemaphoreType.DMA((2, devices)),
                pltpu.SemaphoreType.DMA((2, devices)),
                pltpu.SemaphoreType.DMA((2, devices)),
            ],
            compiler_params=pltpu.CompilerParams(
                collective_id=0, has_side_effects=True, vmem_limit_bytes=56 * 1024 * 1024),
            cost_estimate=pl.CostEstimate(flops=120 * nx * ny * nz, bytes_accessed=16 * nx * ny * nz,
                                          transcendentals=0),
            name="melt_track",
        )(phase, solute, heat_rows, rate_rows, dest_tile, dest_block.reshape(1, rows), active)

    return jax.shard_map(
        on_device,
        mesh=mesh,
        in_specs=(
            P("track", "width", None),
            P("track", "width", None),
            P(("track", "width"), None),
            P(("track", "width"), None),
            P(("track", "width"), None),
            P(("track", "width")),
            P("track", "width"),
        ),
        out_specs=(P("track", "width", None), P("track", "width", None)),
        check_vma=False,
    )
```

time: 203 us -> 60.8 us (0.30)
  other arithmetic: 111 us -> 0 us
  Pallas kernels: 0 us -> 50.7 us
  starting transfers between devices: 48.5 us -> 0 us
  waiting for transfers between devices: 17.7 us -> 0 us
  local copies, waits for them, and re-layouts: 23.2 us -> 8.44 us
    another operation x5 -> x0, other arithmetic: 61 us -> none  [the longest x4 60.9 us: on_device(): jnp.stack([phase, solute])]
    pallas_call x0 -> x1, Pallas kernels: none -> 50.7 us  [on_device(): pl.pallas_call(functools.partial(track_kernel, (tracks, widths, nx, ny, n...]
    ppermute x12 -> x0, starting transfers between devices: 37.6 us -> none  [the longest x6 22.1 us: extended_2(): lax.ppermute(head, axis, [((i + 1) % count, i) for i in range(ends)])]
    concatenate x3 -> x0, other arithmetic: 23.2 us -> none  [extended_2(): jnp.concatenate([lax.ppermute(tail, axis, [(i, (i + 1) % count) for i in...]
    add x2 -> x0, other arithmetic: 18.2 us -> none  [the longest x1 15.1 us: advance(): inner_solute + time_step * (diffusion * laplace(solute_ext, 1.0, 1.0, 1.0...]
    squeeze x3 -> x0, local copies, waits for them, and re-layouts: 17.5 us -> none  [on_device(): phase, solute = advance(extended[0], extended[1], heat, rate, cells, count)]
    ppermute x12 -> x0, waiting for transfers between devices: 15.8 us -> none  [the longest x6 8.03 us: extended_2(): lax.ppermute(tail, axis, [(i, (i + 1) % count) for i in range(ends)])]
    all_to_all x2 -> x0, starting transfers between devices: 10.9 us -> none  [the longest x1 5.84 us: on_device(): lax.all_to_all(outgoing.reshape(devices, CAP, 2 * depth), ('track', 'widt...]
  transfers between devices with their start and end apart: 14 -> 0, of which waited for: 9 -> 0; matrix products, arithmetic and copies ran while one was open for 9% -> 0% of each run, Pallas kernels for 0% -> 0%
where the time goes in v1:
time: 60.8 us; the launch traced here: 59.8 us
  Pallas kernels  50.7 us (83%)
  local copies, waits for them, and re-layouts  8.44 us (14%)
  between operations  0.65 us (1%)
    pallas_call x1, Pallas kernels, on_device(): pl.pallas_call(functools.partial(track_kernel, (tracks, widths, nx, ny, n...  50.7 us
    unnamed x5, local copies, waits for them, and re-layouts  8.44 us

profile of v1, /device:TPU:12, one launch (start us, length us, event | category | flops | bytes accessed | tf_op | source)
XLA Modules:
  0.0 59.8 jit_solution(16745787249063732660)
XLA Ops:
  0.6 1.4 %copy.9.dest_tile = s32[64,1]{1,0:T(8,128)} copy(s32[64,1]{0,1:T(1,128)} %param.11) | data formatting | bytes 512 | tf_op args[4]
  2.0 50.7 %melt_track.1 = (f32[32,64,512]{2,1,0:T(8,128)}, f32[32,64,512]{2,1,0:T(8,128)}) custom-call(f32[32,64,512]{2,1,0:T(8,128)} %phase.1, f32[32,64,512]{2,1,0:T(8,128)} %solute.1, f32[64,512]{1,0:T(8,128)} %heat_rows.1, f32[64,512]{1,0:T(8,128)} %rate_rows.1, s32[64,1]{1,0:T(8,128)} %copy.9.dest_tile, s32[1,64]{1,0:T(1,128)} %bitcast.1, s32[4,8]{1,0:T(4,128)} %active.1), custom_call_target="tpu_custom_call" | custom-call | flops 125829120 | bytes 16777216 | tf_op jit(solution)/shard_map/melt_track/pallas_call | solution.py:360
  52.7 0.0 copy-start
  52.7 5.1 %copy.12 = f32[32,64,512]{2,1,0:T(8,128)} copy(f32[32,64,512]{2,1,0:T(8,128)} %get-tuple-element.4) | data formatting | bytes 8388608
  57.8 0.0 copy-done
  57.8 2.0 %copy.13 = f32[32,64,512]{2,1,0:T(8,128)} copy(f32[32,64,512]{2,1,0:T(8,128)S(1)} %copy-done) | data formatting | bytes 8388608
Async XLA Ops:
  52.7 5.1 %copy-start = (f32[32,64,512]{2,1,0:T(8,128)S(1)}, f32[32,64,512]{2,1,0:T(8,128)}, u32[]{:S(2)}) copy-start(f32[32,64,512]{2,1,0:T(8,128)} %get-tuple-element.5) | copy-start | bytes 12582916

commit v2 on v1

--- a/solution.py
+++ b/solution.py
@@ -10,6 +10,8 @@
 BS = 8
 CAP = 4
 STEPS = 3
+KERNEL_MIB = 30
+LAST_MIB = 20
 LANES = 128
 PAD = 8
 MESH = pl.DeviceIdType.MESH
@@ -25,11 +27,69 @@
 center_solute = 1.0 - 6.0 * time_step * diffusion
 
 
+def depth_sum(tiles):
+    zt_n = len(tiles)
+    lane = lax.broadcasted_iota(jnp.int32, (BS, LANES), 1)
+    first_lane = lane == 0
+    last_lane = lane == LANES - 1
+    up = [pltpu.roll(v, 1, 1) for v in tiles]
+    down = [pltpu.roll(v, LANES - 1, 1) for v in tiles]
+    sums = []
+    for zt in range(zt_n):
+        below = jnp.where(first_lane, up[zt - 1] if zt > 0 else 0.0, up[zt])
+        above = jnp.where(last_lane, down[zt + 1] if zt < zt_n - 1 else 0.0, down[zt])
+        sums.append(below + above)
+    return sums
+
+def cell_block(active, theta, src, dst, shift, count, x, by):
+    zt_n = src.shape[2]
+    x_pad, y_pad = shift
+    there = pl.ds(y_pad + BS * by, BS)
+    bx = x >> 3
+    rate_of = active[bx, by].astype(jnp.float32) * time_step
+    here = pl.ds(PAD + BS * by, BS)
+    back = pl.ds(PAD + BS * by - 1, BS)
+    ahead = pl.ds(PAD + BS * by + 1, BS)
+    p = [src[0, x + 1, zt, here, :] for zt in range(zt_n)]
+    s = [src[1, x + 1, zt, here, :] for zt in range(zt_n)]
+    pz = depth_sum(p)
+    sz = depth_sum(s)
+    for zt in range(zt_n):
+        px = src[0, x, zt, here, :] + src[0, x + 2, zt, here, :]
+        py = src[0, x + 1, zt, back, :] + src[0, x + 1, zt, ahead, :]
+        sx = src[1, x, zt, here, :] + src[1, x + 2, zt, here, :]
+        sy = src[1, x + 1, zt, back, :] + src[1, x + 1, zt, ahead, :]
+        square = p[zt] * p[zt]
+        bond = 1.0 - square
+        drive = coef_track * px + coef_width * py + coef_depth * pz[zt] + p[zt] * (center_phase - square)
+        sink = s[zt] if count == 0 else s[zt] + theta[count - 1, bx, zt, by:by + 1, :]
+        drive = drive - coupling * bond * bond * sink
+        change = rate_of * drive
+        dst[0, x + x_pad, zt, there, :] = p[zt] + change
+        dst[1, x + x_pad, zt, there, :] = (
+            center_solute * s[zt] + (time_step * diffusion) * (sx + sy + sz[zt]) + 0.5 * change)
+
+
+def sweep(block, xs, bys):
+    low_x, high_x, stride = xs
+
+    def body(i, carry):
+        for by in bys:
+            block(low_x + stride * i, by)
+        return carry
+
+    lax.fori_loop(0, (high_x - low_x + stride - 1) // stride, body, 0)
+
+
+def boundary(block, nx, by_n):
+    sweep(block, (0, nx, nx - 1), range(by_n))
+    sweep(block, (1, nx - 1, 1), (0, by_n - 1))
+
+
 def track_kernel(sizes, phase, solute, heat_rows, rate_rows, dest_tile, dest_block, active,
-                 phase_out, solute_out,
-                 f0, f1, y_send, y_recv, label_out, label_in, heat_out, heat_in, rate_out, rate_in,
-                 selector, theta,
-                 load_sem, store_sem, x_send_sem, x_recv_sem, y_send_sem, y_recv_sem,
+                 f0, f1, theta, y_send, y_recv, label_out, label_in, heat_out, heat_in, rate_out, rate_in,
+                 selector,
+                 load_sem, x_send_sem, x_recv_sem, y_send_sem, y_recv_sem,
                  label_sems, heat_sems, rate_sems):
     tracks, widths, nx, ny, nz, rows = sizes
     devices = tracks * widths
@@ -66,9 +126,9 @@
 
     lax.fori_loop(1, devices, greet, 0)
 
-    tcol = dest_tile[...].astype(jnp.float32)
+    trow = dest_tile[...].astype(jnp.float32)
     eye = lax.broadcasted_iota(jnp.int32, (rows, rows), 0) == lax.broadcasted_iota(jnp.int32, (rows, rows), 1)
-    trow = jnp.sum(jnp.where(eye, tcol, 0.0), axis=0, keepdims=True)
+    tcol = jnp.sum(jnp.where(eye, trow, 0.0), axis=1, keepdims=True)
     before = lax.broadcasted_iota(jnp.int32, (rows, rows), 0) < lax.broadcasted_iota(jnp.int32, (rows, rows), 1)
     rank = jnp.sum(jnp.where(before & (tcol == trow), 1.0, 0.0), axis=0, keepdims=True)
     slot = trow * CAP + rank
@@ -195,45 +255,6 @@
 
         lax.fori_loop(0, nx, unpack, 0)
 
-    lane = lax.broadcasted_iota(jnp.int32, (BS, LANES), 1)
-    first_lane = lane == 0
-    last_lane = lane == LANES - 1
-
-    def depth_sum(tiles):
-        up = [pltpu.roll(v, 1, 1) for v in tiles]
-        down = [pltpu.roll(v, LANES - 1, 1) for v in tiles]
-        sums = []
-        for zt in range(zt_n):
-            below = jnp.where(first_lane, up[zt - 1] if zt > 0 else 0.0, up[zt])
-            above = jnp.where(last_lane, down[zt + 1] if zt < zt_n - 1 else 0.0, down[zt])
-            sums.append(below + above)
-        return sums
-
-    def cell_block(src, dst, count, x, by):
-        bx = x >> 3
-        rate_of = active[bx, by].astype(jnp.float32) * time_step
-        here = pl.ds(PAD + BS * by, BS)
-        back = pl.ds(PAD + BS * by - 1, BS)
-        ahead = pl.ds(PAD + BS * by + 1, BS)
-        p = [src[0, x + 1, zt, here, :] for zt in range(zt_n)]
-        s = [src[1, x + 1, zt, here, :] for zt in range(zt_n)]
-        pz = depth_sum(p)
-        sz = depth_sum(s)
-        for zt in range(zt_n):
-            px = src[0, x, zt, here, :] + src[0, x + 2, zt, here, :]
-            py = src[0, x + 1, zt, back, :] + src[0, x + 1, zt, ahead, :]
-            sx = src[1, x, zt, here, :] + src[1, x + 2, zt, here, :]
-            sy = src[1, x + 1, zt, back, :] + src[1, x + 1, zt, ahead, :]
-            square = p[zt] * p[zt]
-            bond = 1.0 - square
-            drive = coef_track * px + coef_width * py + coef_depth * pz[zt] + p[zt] * (center_phase - square)
-            sink = s[zt] if count == 0 else s[zt] + theta[count - 1, bx, zt, by:by + 1, :]
-            drive = drive - coupling * bond * bond * sink
-            change = rate_of * drive
-            dst[0, x + 1, zt, here, :] = p[zt] + change
-            dst[1, x + 1, zt, here, :] = (
-                center_solute * s[zt] + (time_step * diffusion) * (sx + sy + sz[zt]) + 0.5 * change)
-
     def heat_block(src, dst, x, by):
         bx = x >> 3
         rate_of = active[bx, by].astype(jnp.float32) * (time_step * coupling)
@@ -245,22 +266,7 @@
             dst[0, x + 1, zt, here, :] = dst[0, x + 1, zt, here, :] - change
             dst[1, x + 1, zt, here, :] = dst[1, x + 1, zt, here, :] - 0.5 * change
 
-    def sweep(block, xs, bys):
-        low_x, high_x, stride = xs
-
-        def body(i, carry):
-            for by in bys:
-                block(low_x + stride * i, by)
-            return carry
-
-        lax.fori_loop(0, (high_x - low_x + stride - 1) // stride, body, 0)
-
     inner = range(1, by_n - 1)
-    outer = (0, by_n - 1)
-
-    def boundary(block):
-        sweep(block, (0, nx, nx - 1), range(by_n))
-        sweep(block, (1, nx - 1, 1), outer)
 
     def arrived(rows_in):
         both = jnp.concatenate([rows_in[:, j].reshape(8 * devices, LANES) for j in range(pairs)], axis=1)
@@ -276,14 +282,14 @@
     send_halo(f0, 0)
     send_all(rate_x)
 
-    step0 = functools.partial(cell_block, f0, f1, 0)
-    step1 = functools.partial(cell_block, f1, f0, 1)
-    step2 = functools.partial(cell_block, f0, f1, 2)
+    step0 = functools.partial(cell_block, active, theta, f0, f1, (1, PAD), 0)
+    step1 = functools.partial(cell_block, active, theta, f1, f0, (1, PAD), 1)
+    step2 = functools.partial(cell_block, active, theta, f0, f1, (1, PAD), 2)
     finish = functools.partial(heat_block, f0, f1)
 
     sweep(step0, (1, nx - 1, 1), inner)
     wait_halo(f0, 0)
-    boundary(step0)
+    boundary(step0, nx, by_n)
 
     wait_all(labels_x, heat_x)
     spread = jnp.where(diagonal, jnp.broadcast_to(label_in[...], (devices, 8, LANES)), 0.0)
@@ -296,7 +302,7 @@
         for zt in range(zt_n):
             theta[0, bx, zt] = tile_of(heat, bx, zt)
 
-    boundary(finish)
+    boundary(finish, nx, by_n)
     send_halo(f1, 1)
     sweep(finish, (1, nx - 1, 1), inner)
 
@@ -312,31 +318,53 @@
     half = nx // 2
     sweep(step1, (1, half, 1), inner)
     wait_halo(f1, 1)
-    boundary(step1)
+    boundary(step1, nx, by_n)
     send_halo(f0, 2)
     sweep(step1, (half, nx - 1, 1), inner)
-    sweep(step2, (1, nx - 1, 1), inner)
-
-    def stores(part, x_at, x_len, y_at, y_len):
+    sweep(step2, (1, half, 1), inner)
+    wait_halo(f0, 2)
+
+
+def last_kernel(active, f0, f1, theta, phase_out, solute_out, late, store_sem):
+    zt_n = f0.shape[2]
+    nx, ny, _ = phase_out.shape
+    by_n = ny // BS
+    half = nx // 2
+
+    def stores(part, src, shift, x_at, x_len, y_at, y_len):
+        x_pad, y_pad = shift
         out = []
         for f, ref in enumerate((phase_out, solute_out)):
             for zt in range(zt_n):
                 out.append(pltpu.make_async_copy(
-                    f1.at[f, pl.ds(1 + x_at, x_len), zt, pl.ds(PAD + y_at, y_len), :],
+                    src.at[f, pl.ds(x_pad + x_at, x_len), zt, pl.ds(y_pad + y_at, y_len), :],
                     ref.at[pl.ds(x_at, x_len), pl.ds(y_at, y_len), pl.ds(zt * LANES, LANES)],
                     store_sem.at[part, f, zt]))
         return out
 
-    middle = stores(0, 1, nx - 2, BS, ny - 2 * BS)
-    for copy in middle:
-        copy.start()
-    wait_halo(f0, 2)
-    boundary(step2)
-    rim = (stores(1, 0, 1, 0, ny) + stores(2, nx - 1, 1, 0, ny)
-           + stores(3, 1, nx - 2, 0, BS) + stores(4, 1, nx - 2, ny - BS, BS))
-    for copy in rim:
-        copy.start()
-    for copy in middle + rim:
+    started = []
+
+    def start(*where):
+        copies = stores(len(started) // (2 * zt_n), *where)
+        for copy in copies:
+            copy.start()
+        started.extend(copies)
+
+    start(f1, (1, PAD), 1, half - 1, BS, ny - 2 * BS)
+    step = functools.partial(cell_block, active, theta, f0, late, (0, 0), 2)
+    ends = (0, by_n - 1)
+    sweep(step, (0, half, nx), range(by_n))
+    sweep(step, (1, half, 1), ends)
+    start(late, (0, 0), 0, 1, 0, ny)
+    start(late, (0, 0), 1, half - 1, 0, BS)
+    start(late, (0, 0), 1, half - 1, ny - BS, BS)
+    pieces = 4
+    width = (nx - half) // pieces
+    for piece in range(pieces):
+        at = half + piece * width
+        sweep(step, (at, at + width, 1), range(by_n))
+        start(late, (0, 0), at, width, 0, ny)
+    for copy in started:
         copy.wait()
 
 
@@ -357,18 +385,17 @@
         moved = pltpu.VMEM((devices, pairs, 8, LANES), f32)
         vmem = pl.BlockSpec(memory_space=pltpu.VMEM)
         any_space = pl.BlockSpec(memory_space=pl.ANY)
-        return pl.pallas_call(
+        smem = pl.BlockSpec(memory_space=pltpu.SMEM)
+        tables = pltpu.VMEM((2, nx // BS, zt_n, ny // BS, LANES), f32)
+        f0, f1, theta = pl.pallas_call(
             functools.partial(track_kernel, (tracks, widths, nx, ny, nz, rows)),
-            out_shape=(jax.ShapeDtypeStruct(phase.shape, f32), jax.ShapeDtypeStruct(solute.shape, f32)),
-            in_specs=[any_space, any_space, vmem, vmem, vmem, vmem,
-                      pl.BlockSpec(memory_space=pltpu.SMEM)],
-            out_specs=(any_space, any_space),
+            out_shape=(field, field, tables),
+            in_specs=[any_space, any_space, vmem, vmem, vmem, vmem, smem],
+            out_specs=(vmem, vmem, vmem),
             scratch_shapes=[
-                field, field, ends, ends, label, label, moved, moved, moved, moved,
+                ends, ends, label, label, moved, moved, moved, moved,
                 pltpu.VMEM((8 * devices, LANES), f32),
-                pltpu.VMEM((2, nx // BS, zt_n, ny // BS, LANES), f32),
                 pltpu.SemaphoreType.DMA((2, zt_n)),
-                pltpu.SemaphoreType.DMA((5, 2, zt_n)),
                 pltpu.SemaphoreType.DMA((STEPS, 2)),
                 pltpu.SemaphoreType.DMA((STEPS, 2)),
                 pltpu.SemaphoreType.DMA((STEPS, 2)),
@@ -378,11 +405,25 @@
                 pltpu.SemaphoreType.DMA((2, devices)),
             ],
             compiler_params=pltpu.CompilerParams(
-                collective_id=0, has_side_effects=True, vmem_limit_bytes=56 * 1024 * 1024),
-            cost_estimate=pl.CostEstimate(flops=120 * nx * ny * nz, bytes_accessed=16 * nx * ny * nz,
+                collective_id=0, has_side_effects=True, vmem_limit_bytes=KERNEL_MIB * 1024 * 1024),
+            cost_estimate=pl.CostEstimate(flops=90 * nx * ny * nz, bytes_accessed=8 * nx * ny * nz,
                                           transcendentals=0),
             name="melt_track",
-        )(phase, solute, heat_rows, rate_rows, dest_tile, dest_block.reshape(1, rows), active)
+        )(phase, solute, heat_rows, rate_rows, dest_tile.reshape(1, rows), dest_block.reshape(1, rows), active)
+        return pl.pallas_call(
+            last_kernel,
+            out_shape=(jax.ShapeDtypeStruct(phase.shape, f32), jax.ShapeDtypeStruct(solute.shape, f32)),
+            in_specs=[smem, vmem, vmem, vmem],
+            out_specs=(any_space, any_space),
+            scratch_shapes=[
+                pltpu.VMEM((2, nx, zt_n, ny, LANES), f32),
+                pltpu.SemaphoreType.DMA((8, 2, zt_n)),
+            ],
+            compiler_params=pltpu.CompilerParams(vmem_limit_bytes=LAST_MIB * 1024 * 1024),
+            cost_estimate=pl.CostEstimate(flops=30 * nx * ny * nz, bytes_accessed=8 * nx * ny * nz,
+                                          transcendentals=0),
+            name="melt_last",
+        )(active, f0, f1, theta)
 
     return jax.shard_map(
         on_device,

time: 60.8 us -> 56.4 us (0.928); the launches traced: 59.8 us -> 56.2 us
  local copies, waits for them, and re-layouts: 8.44 us -> 3.79 us
  Pallas kernels: 50.7 us -> 51.7 us
    pallas_call x0 -> x1, Pallas kernels: none -> 7.57 us  [on_device(): pl.pallas_call(last_kernel, out_shape=(jax.ShapeDtypeStruct(phase.shape,...]
    pallas_call x1, Pallas kernels: 50.7 us -> 44.2 us  [on_device(): pl.pallas_call(functools.partial(track_kernel, (tracks, widths, nx, ny, n...]
    unnamed x5 -> x10, local copies, waits for them, and re-layouts: 8.44 us -> 3.79 us
where the time goes in v2:
time: 56.4 us; the launch traced here: 56.2 us
  Pallas kernels  51.7 us (92%)
  local copies, waits for them, and re-layouts  3.79 us (7%)
  between operations  0.65 us (1%)
    pallas_call x1, Pallas kernels, on_device(): pl.pallas_call(functools.partial(track_kernel, (tracks, widths, nx, ny, n...  44.2 us
    pallas_call x1, Pallas kernels, on_device(): pl.pallas_call(last_kernel, out_shape=(jax.ShapeDtypeStruct(phase.shape,...  7.57 us
    unnamed x10, local copies, waits for them, and re-layouts  3.79 us

profile of v2, /device:TPU:12, one launch (start us, length us, event | category | flops | bytes accessed | tf_op | source)
XLA Modules:
  0.0 56.2 jit_solution(13916742034270257197)
XLA Ops:
  0.6 0.0 copy-start
  0.6 0.9 %copy-done = f32[64,512]{1,0:T(8,128)S(1)} copy-done((f32[64,512]{1,0:T(8,128)S(1)}, f32[64,512]{1,0:T(8,128)}, u32[]{:S(2)}) %copy-start) | copy-done | bytes 131096
  1.5 0.0 copy-start.1
  1.5 0.9 %copy-done.1 = f32[64,512]{1,0:T(8,128)S(1)} copy-done((f32[64,512]{1,0:T(8,128)S(1)}, f32[64,512]{1,0:T(8,128)}, u32[]{:S(2)}) %copy-start.1) | copy-done | bytes 131096
  2.4 0.0 copy-start.2
  2.4 0.7 %copy-done.2 = s32[4,8]{1,0:T(4,128)S(1)} copy-done((s32[4,8]{1,0:T(4,128)S(1)}, s32[4,8]{1,0:T(4,128)}, u32[]{:S(2)}) %copy-start.2) | copy-done | bytes 152
  3.1 0.0 copy-start.3
  3.1 0.7 %copy-done.3 = s32[64,1]{0,1:T(1,128)S(1)} copy-done((s32[64,1]{0,1:T(1,128)S(1)}, s32[64,1]{0,1:T(1,128)}, u32[]{:S(2)}) %copy-start.3) | copy-done | bytes 280
  3.8 0.0 copy-start.4
  3.8 0.7 %copy-done.4 = s32[64]{0:T(128)S(1)} copy-done((s32[64]{0:T(128)S(1)}, s32[64]{0:T(128)}, u32[]{:S(2)}) %copy-start.4) | copy-done | bytes 280
  4.4 44.2 %melt_track.1 = (f32[2,34,4,80,128]{4,3,2,1,0:T(8,128)S(1)}, f32[2,34,4,80,128]{4,3,2,1,0:T(8,128)S(1)}, f32[2,4,4,8,128]{4,3,2,1,0:T(8,128)S(1)}) custom-call(f32[32,64,512]{2,1,0:T(8,128)} %phase.1, f32[32,64,512]{2,1,0:T(8,128)} %solute.1, f32[64,512]{1,0:T(8,128)S(1)} %copy-done, f32[64,512]{1,0:T(8,128)S(1)} %copy-done.1, s32[1,64]{1,0:T(1,128)S(1)} %bitcast.2, ...), custom_call_target="tpu_custom_call" | custom-call | flops 94371840 | bytes 8388608 | tf_op jit(solution)/shard_map/melt_track/pallas_call | solution.py:390
  48.6 7.6 %melt_last.1 = (f32[32,64,512]{2,1,0:T(8,128)}, f32[32,64,512]{2,1,0:T(8,128)}) custom-call(s32[4,8]{1,0:T(4,128)S(1)} %copy-done.2, f32[2,34,4,80,128]{4,3,2,1,0:T(8,128)S(1)} %get-tuple-element.5.f0, f32[2,34,4,80,128]{4,3,2,1,0:T(8,128)S(1)} %get-tuple-element.6.f1, f32[2,4,4,8,128]{4,3,2,1,0:T(8,128)S(1)} %get-tuple-element.7.theta), custom_call_target="tpu_custom_call" | custom-call | flops 31457280 | bytes 8388608 | tf_op jit(solution)/shard_map/melt_last/pallas_call | solution.py:413
Async XLA Ops:
  0.6 0.9 %copy-start = (f32[64,512]{1,0:T(8,128)S(1)}, f32[64,512]{1,0:T(8,128)}, u32[]{:S(2)}) copy-start(f32[64,512]{1,0:T(8,128)} %heat_rows.1) | copy-start | bytes 393220
  1.5 0.9 %copy-start.1 = (f32[64,512]{1,0:T(8,128)S(1)}, f32[64,512]{1,0:T(8,128)}, u32[]{:S(2)}) copy-start(f32[64,512]{1,0:T(8,128)} %rate_rows.1) | copy-start | bytes 393220
  2.4 0.7 %copy-start.2 = (s32[4,8]{1,0:T(4,128)S(1)}, s32[4,8]{1,0:T(4,128)}, u32[]{:S(2)}) copy-start(s32[4,8]{1,0:T(4,128)} %active.3) | copy-start | bytes 388
  3.1 0.7 %copy-start.3 = (s32[64,1]{0,1:T(1,128)S(1)}, s32[64,1]{0,1:T(1,128)}, u32[]{:S(2)}) copy-start(s32[64,1]{0,1:T(1,128)} %param.11) | copy-start | bytes 772
  3.8 0.7 %copy-start.4 = (s32[64]{0:T(128)S(1)}, s32[64]{0:T(128)}, u32[]{:S(2)}) copy-start(s32[64]{0:T(128)} %param.12) | copy-start | bytes 772

commit v3 on v2

--- a/solution.py
+++ b/solution.py
@@ -10,7 +10,7 @@
 BS = 8
 CAP = 4
 STEPS = 3
-KERNEL_MIB = 30
+KERNEL_MIB = 42
 LAST_MIB = 20
 LANES = 128
 PAD = 8
@@ -86,10 +86,10 @@
     sweep(block, (1, nx - 1, 1), (0, by_n - 1))
 
 
-def track_kernel(sizes, phase, solute, heat_rows, rate_rows, dest_tile, dest_block, active,
+def track_kernel(sizes, phase, solute, heat_hbm, rate_hbm, tile_hbm, block_hbm, active,
                  f0, f1, theta, y_send, y_recv, label_out, label_in, heat_out, heat_in, rate_out, rate_in,
-                 selector,
-                 load_sem, x_send_sem, x_recv_sem, y_send_sem, y_recv_sem,
+                 selector, heat_rows, rate_rows, dest_tile, dest_block,
+                 load_sem, small_sem, x_send_sem, x_recv_sem, y_send_sem, y_recv_sem,
                  label_sems, heat_sems, rate_sems):
     tracks, widths, nx, ny, nz, rows = sizes
     devices = tracks * widths
@@ -111,6 +111,10 @@
                     load_sem.at[f, zt]))
         return out
 
+    small = [pltpu.make_async_copy(source, target, small_sem.at[i]) for i, (source, target) in enumerate(
+        ((tile_hbm, dest_tile), (block_hbm, dest_block), (heat_hbm, heat_rows), (rate_hbm, rate_rows)))]
+    for copy in small:
+        copy.start()
     for copy in loads():
         copy.start()
 
@@ -125,6 +129,9 @@
         return carry
 
     lax.fori_loop(1, devices, greet, 0)
+
+    for copy in small:
+        copy.wait()
 
     trow = dest_tile[...].astype(jnp.float32)
     eye = lax.broadcasted_iota(jnp.int32, (rows, rows), 0) == lax.broadcasted_iota(jnp.int32, (rows, rows), 1)
@@ -150,7 +157,6 @@
             target[:, j] = jnp.where(low, first, second).reshape(devices, 8, LANES)
 
     pack_rows(heat_rows, heat_out)
-    pack_rows(rate_rows, rate_out)
 
     has = (t > 0, t < tracks - 1, w > 0, w < widths - 1)
     for side in range(2):
@@ -228,7 +234,7 @@
                         y_send[stage, side, f, x, zt] = field[f, x + 1, zt, pl.ds(row, 1), :]
             return carry
 
-        lax.fori_loop(0, nx, pack, 0)
+        lax.fori_loop(0, nx, pack, 0, unroll=4)
         for side in range(2):
             @pl.when(has[2 + side])
             def _():
@@ -253,7 +259,7 @@
                         field[f, x + 1, zt, pl.ds(row, 1), :] = y_recv[stage, side, f, x, zt]
             return carry
 
-        lax.fori_loop(0, nx, unpack, 0)
+        lax.fori_loop(0, nx, unpack, 0, unroll=4)
 
     def heat_block(src, dst, x, by):
         bx = x >> 3
@@ -280,6 +286,7 @@
     for copy in loads():
         copy.wait()
     send_halo(f0, 0)
+    pack_rows(rate_rows, rate_out)
     send_all(rate_x)
 
     step0 = functools.partial(cell_block, active, theta, f0, f1, (1, PAD), 0)
@@ -386,16 +393,22 @@
         vmem = pl.BlockSpec(memory_space=pltpu.VMEM)
         any_space = pl.BlockSpec(memory_space=pl.ANY)
         smem = pl.BlockSpec(memory_space=pltpu.SMEM)
+        hbm = pl.BlockSpec(memory_space=pltpu.HBM)
         tables = pltpu.VMEM((2, nx // BS, zt_n, ny // BS, LANES), f32)
         f0, f1, theta = pl.pallas_call(
             functools.partial(track_kernel, (tracks, widths, nx, ny, nz, rows)),
             out_shape=(field, field, tables),
-            in_specs=[any_space, any_space, vmem, vmem, vmem, vmem, smem],
+            in_specs=[hbm] * 6 + [smem],
             out_specs=(vmem, vmem, vmem),
             scratch_shapes=[
                 ends, ends, label, label, moved, moved, moved, moved,
                 pltpu.VMEM((8 * devices, LANES), f32),
+                pltpu.VMEM((rows, nz), f32),
+                pltpu.VMEM((rows, nz), f32),
+                pltpu.VMEM((1, rows), jnp.int32),
+                pltpu.VMEM((1, rows), jnp.int32),
                 pltpu.SemaphoreType.DMA((2, zt_n)),
+                pltpu.SemaphoreType.DMA((4,)),
                 pltpu.SemaphoreType.DMA((STEPS, 2)),
                 pltpu.SemaphoreType.DMA((STEPS, 2)),
                 pltpu.SemaphoreType.DMA((STEPS, 2)),

time: 56.4 us -> 52.1 us (0.924)
  local copies, waits for them, and re-layouts: 3.79 us -> 0.01 us
    unnamed x10 -> x2, local copies, waits for them, and re-layouts: 3.79 us -> 0.01 us
where the time goes in v3:
time: 52.1 us; the launch traced here: 51.9 us
  Pallas kernels  51.3 us (98%)
  between operations  0.66 us (1%)
    pallas_call x1, Pallas kernels, on_device(): pl.pallas_call(functools.partial(track_kernel, (tracks, widths, nx, ny, n...  43.9 us
    pallas_call x1, Pallas kernels, on_device(): pl.pallas_call(last_kernel, out_shape=(jax.ShapeDtypeStruct(phase.shape,...  7.38 us

profile of v3, /device:TPU:12, one launch (start us, length us, event | category | flops | bytes accessed | tf_op | source)
XLA Modules:
  0.0 51.9 jit_solution(1962308662185550265)
XLA Ops:
  0.6 0.0 copy-start
  0.6 43.9 %melt_track.1 = (f32[2,34,4,80,128]{4,3,2,1,0:T(8,128)S(1)}, f32[2,34,4,80,128]{4,3,2,1,0:T(8,128)S(1)}, f32[2,4,4,8,128]{4,3,2,1,0:T(8,128)S(1)}) custom-call(f32[32,64,512]{2,1,0:T(8,128)} %phase.1, f32[32,64,512]{2,1,0:T(8,128)} %solute.1, f32[64,512]{1,0:T(8,128)} %heat_hbm.1, f32[64,512]{1,0:T(8,128)} %rate_hbm.1, s32[1,64]{1,0:T(1,128)} %bitcast.2, ...), custom_call_target="tpu_custom_call" | custom-call | flops 94371840 | bytes 8388608 | tf_op jit(solution)/shard_map/melt_track/pallas_call | solution.py:398
  44.6 0.0 copy-done
  44.6 7.4 %melt_last.1 = (f32[32,64,512]{2,1,0:T(8,128)}, f32[32,64,512]{2,1,0:T(8,128)}) custom-call(s32[4,8]{1,0:T(4,128)S(1)} %copy-done, f32[2,34,4,80,128]{4,3,2,1,0:T(8,128)S(1)} %get-tuple-element.5.f0, f32[2,34,4,80,128]{4,3,2,1,0:T(8,128)S(1)} %get-tuple-element.6.f1, f32[2,4,4,8,128]{4,3,2,1,0:T(8,128)S(1)} %get-tuple-element.7.theta), custom_call_target="tpu_custom_call" | custom-call | flops 31457280 | bytes 8388608 | tf_op jit(solution)/shard_map/melt_last/pallas_call | solution.py:426
Async XLA Ops:
  0.6 43.9 %copy-start = (s32[4,8]{1,0:T(4,128)S(1)}, s32[4,8]{1,0:T(4,128)}, u32[]{:S(2)}) copy-start(s32[4,8]{1,0:T(4,128)} %active.3) | copy-start | bytes 388

commit v4 on v3

--- a/solution.py
+++ b/solution.py
@@ -323,11 +323,12 @@
             theta[1, bx, zt] = whole - (2 * time_step) * slope
 
     half = nx // 2
-    sweep(step1, (1, half, 1), inner)
+    early = nx // 4
+    sweep(step1, (1, early, 1), inner)
     wait_halo(f1, 1)
     boundary(step1, nx, by_n)
     send_halo(f0, 2)
-    sweep(step1, (half, nx - 1, 1), inner)
+    sweep(step1, (early, nx - 1, 1), inner)
     sweep(step2, (1, half, 1), inner)
     wait_halo(f0, 2)
 

time: 52.1 us -> 52.4 us (level)
  no operation moved by 1% of the time
where the time goes in v4:
time: 52.4 us; the launch traced here: 51.9 us
  Pallas kernels  51.3 us (98%)
  between operations  0.66 us (1%)
    pallas_call x1, Pallas kernels, on_device(): pl.pallas_call(functools.partial(track_kernel, (tracks, widths, nx, ny, n...  43.9 us
    pallas_call x1, Pallas kernels, on_device(): pl.pallas_call(last_kernel, out_shape=(jax.ShapeDtypeStruct(phase.shape,...  7.38 us

profile of v4, /device:TPU:12, one launch (start us, length us, event | category | flops | bytes accessed | tf_op | source)
XLA Modules:
  0.0 51.9 jit_solution(4907746729182303530)
XLA Ops:
  0.6 0.0 copy-start
  0.6 43.9 %melt_track.1 = (f32[2,34,4,80,128]{4,3,2,1,0:T(8,128)S(1)}, f32[2,34,4,80,128]{4,3,2,1,0:T(8,128)S(1)}, f32[2,4,4,8,128]{4,3,2,1,0:T(8,128)S(1)}) custom-call(f32[32,64,512]{2,1,0:T(8,128)} %phase.1, f32[32,64,512]{2,1,0:T(8,128)} %solute.1, f32[64,512]{1,0:T(8,128)} %heat_hbm.1, f32[64,512]{1,0:T(8,128)} %rate_hbm.1, s32[1,64]{1,0:T(1,128)} %bitcast.2, ...), custom_call_target="tpu_custom_call" | custom-call | flops 94371840 | bytes 8388608 | tf_op jit(solution)/shard_map/melt_track/pallas_call | solution.py:399
  44.6 0.0 copy-done
  44.6 7.4 %melt_last.1 = (f32[32,64,512]{2,1,0:T(8,128)}, f32[32,64,512]{2,1,0:T(8,128)}) custom-call(s32[4,8]{1,0:T(4,128)S(1)} %copy-done, f32[2,34,4,80,128]{4,3,2,1,0:T(8,128)S(1)} %get-tuple-element.5.f0, f32[2,34,4,80,128]{4,3,2,1,0:T(8,128)S(1)} %get-tuple-element.6.f1, f32[2,4,4,8,128]{4,3,2,1,0:T(8,128)S(1)} %get-tuple-element.7.theta), custom_call_target="tpu_custom_call" | custom-call | flops 31457280 | bytes 8388608 | tf_op jit(solution)/shard_map/melt_last/pallas_call | solution.py:427
Async XLA Ops:
  0.6 43.9 %copy-start = (s32[4,8]{1,0:T(4,128)S(1)}, s32[4,8]{1,0:T(4,128)}, u32[]{:S(2)}) copy-start(s32[4,8]{1,0:T(4,128)} %active.3) | copy-start | bytes 388
